TPU v7x, 32 devices: a whole 2x2x4 slice. The times are simulated.
32 devices in a mesh: chan: 8 (over z, core), win: 4 (over y, x).
Axes of the slice: x: 2, y: 2, z: 4, core: 2. Of those that a mesh axis runs over, the one named last changes fastest.
Arguments:
- series: bfloat16 [32, 2048, 1500], P('win', 'chan'), may hold values from -1700 to 1700
- validity: int32 [32, 2048], P('win', 'chan'), may hold values from 0 to 1, as said below
Outputs:
- source_gathers: float32 [2048, 8, 4, 64, 128], P('chan', None, 'win')
Inputs may be any that keep to these rules, and one draw needn't show every extreme that they name: `validity`: a channel flagged dead is 0 in every window.
All inputs are finite; a program needn't handle non-finite values.
Results may differ from a plain program's by a relative error of at most 0.0037.
Values may be sent and summed in bfloat16 or wider, within the bound.
A program may use at most 448 MiB of HBM per device.

v0:
```python
import functools
import math

import jax
import jax.numpy as jnp
import ml_dtypes
import numpy as np
from jax import lax
from jax.experimental import pallas as pl
from jax.experimental.pallas import tpu as pltpu
from jax.sharding import PartitionSpec as P

BINS = 128
LAGS = 128
LOWEST_BIN = 6


def build_tables(samples):
    t = np.arange(samples)
    k = np.arange(BINS) + LOWEST_BIN
    step = 2.0 * math.pi / samples
    angle = (t[:, None] * k[None, :] % samples) * step
    hann = 0.5 - 0.5 * np.cos(t * step)
    taper = np.concatenate(
        [hann[:, None] * np.cos(angle), -hann[:, None] * np.sin(angle)], axis=1
    )
    lag = np.arange(LAGS) - LAGS // 2
    lag_angle = (k[:, None] * lag[None, :] % samples) * step
    inverse = np.concatenate([np.cos(lag_angle), -np.sin(lag_angle)], axis=0)
    to_half = lambda x: x.astype(np.float32).astype(ml_dtypes.bfloat16)
    return to_half(taper), to_half(inverse)


def pair_kernel(src_ref, recv_ref, scale_ref, inv_ref, out_ref, cross):
    bins, _, sc, depth = src_ref.shape
    ti = recv_ref.shape[2]
    slot = out_ref.shape[3]
    halves = ti // 128

    def bin_step(k, carry):
        r = recv_ref[k]
        l = src_ref[k].reshape(2 * sc, depth)
        x = jnp.dot(l, r, preferred_element_type=jnp.float32)
        for h in range(halves):
            part = x[:, h * 128 : (h + 1) * 128]
            cross[h, pl.ds(pl.multiple_of(k * sc, sc), sc), :] = part[:sc]
            cross[h, pl.ds(pl.multiple_of((bins + k) * sc, sc), sc), :] = part[sc:]
        return carry

    lax.fori_loop(0, bins, bin_step, 0, unroll=8)

    inv = inv_ref[...]
    per = 128 // slot

    def source_step(s, carry):
        for h in range(halves):
            x = cross[h, pl.ds(s, 2 * bins, stride=sc), :]
            x = x * scale_ref[s][:, h * 128 : (h + 1) * 128]
            y = lax.dot_general(
                x.astype(jnp.bfloat16),
                inv,
                (((0,), (0,)), ((), ())),
                preferred_element_type=jnp.float32,
            )
            out_ref[s, h * per : (h + 1) * per, 0] = y.reshape(per, slot, LAGS)
        return carry

    lax.fori_loop(0, sc, source_step, 0, unroll=4)


def pair_block(src, recv, scale, inverse, slot):
    bins, _, sources, depth = src.shape
    receivers = recv.shape[2]
    sc = min(64, sources)
    ti = min(256, receivers)
    return pl.pallas_call(
        pair_kernel,
        grid=(receivers // ti, sources // sc),
        in_specs=[
            pl.BlockSpec((bins, 2, sc, depth), lambda i, s: (0, 0, s, 0)),
            pl.BlockSpec((bins, depth, ti), lambda i, s: (0, 0, i)),
            pl.BlockSpec((sc, 1, ti), lambda i, s: (s, 0, i)),
            pl.BlockSpec((2 * bins, LAGS), lambda i, s: (0, 0)),
        ],
        out_specs=pl.BlockSpec(
            (sc, ti // slot, 1, slot, LAGS), lambda i, s: (s, i, 0, 0, 0)
        ),
        out_shape=jax.ShapeDtypeStruct(
            (sources, receivers // slot, 1, slot, LAGS), jnp.float32
        ),
        scratch_shapes=[pltpu.VMEM((ti // 128, 2 * bins * sc, 128), jnp.float32)],
        compiler_params=pltpu.CompilerParams(vmem_limit_bytes=58 * 1024 * 1024),
        cost_estimate=pl.CostEstimate(
            flops=2 * sources * receivers * 2 * bins * (depth + LAGS),
            bytes_accessed=sources * receivers * LAGS * 4,
            transcendentals=0,
        ),
        name="pairs",
    )(src, recv, scale[:, None, :], inverse)


def on_device(series, validity):
    win_rows, channels, samples = series.shape
    taper, inverse = build_tables(samples)
    spectra = jnp.dot(
        series.reshape(win_rows * channels, samples),
        jnp.asarray(taper),
        preferred_element_type=jnp.float32,
    ).reshape(win_rows, channels, 2 * BINS)
    energy = jnp.mean(spectra * spectra, axis=-1, keepdims=True)
    flag_float = validity.astype(jnp.float32)
    whitened = (spectra * lax.rsqrt(energy + 1e-06) * flag_float[..., None]).astype(jnp.bfloat16)
    flags = validity.astype(jnp.bfloat16)

    blocks = lax.axis_size("chan")
    slots = lax.axis_size("win")
    slot = channels // slots
    v = lax.axis_index("win")

    src = lax.all_gather(whitened, "win", axis=0, tiled=True)
    windows = src.shape[0]
    own = lax.dynamic_slice_in_dim(src, v * slot, slot, axis=1)
    recv = lax.all_gather(own, "chan", axis=1, tiled=True)
    src_flags = lax.all_gather(flags, "win", axis=0, tiled=True)
    own_flags = lax.dynamic_slice_in_dim(src_flags, v * slot, slot, axis=1)
    recv_flags = lax.all_gather(own_flags, "chan", axis=1, tiled=True)
    count = jnp.einsum("ws,wi->si", src_flags, recv_flags, preferred_element_type=jnp.float32)
    scale = 1.0 / jnp.maximum(count, 1.0)

    s4 = src.reshape(windows, channels, 2, BINS).transpose(3, 2, 1, 0)
    real, imag = s4[:, 0], s4[:, 1]
    src_l = jnp.stack(
        [jnp.concatenate([real, imag], -1), jnp.concatenate([-imag, real], -1)], axis=1
    )
    receivers = blocks * slot
    recv_r = recv.reshape(windows, receivers, 2, BINS).transpose(3, 2, 0, 1)
    recv_r = recv_r.reshape(BINS, 2 * windows, receivers)
    return pair_block(src_l, recv_r, scale, jnp.asarray(inverse), slot)


def solution(mesh):
    return jax.shard_map(
        on_device,
        mesh=mesh,
        in_specs=(P("win", "chan", None), P("win", "chan")),
        out_specs=P("chan", None, "win", None, None),
        check_vma=False,
    )
```

profile of v0, /device:TPU:0, one launch (start us, length us, event | category | flops | bytes accessed | tf_op | source)
XLA Modules:
  0.0 407.4 jit_solution(4491066953445736159)
XLA Ops:
  6.5 0.8 fusion.6
  7.3 4.8 %multiply_reduce_fusion = (f32[8,256]{1,0:T(8,128)S(1)}, f32[256,8,256]{2,0,1:T(8,128)S(1)}) fusion(bf16[1500,256,1]{1,0,2:T(8,128)(2,1)} %constant.25, bf16[8,256,1500]{1,0,2:T(8,128)(2,1)} %param.4), kind=kOutput, calls=%fused_computation.8 | convolution fusion | flops 1573910528 | bytes 9017344 | tf_op jit(solution)/shard_map/dot_general | solution.py:105
  12.2 0.2 fusion.4
  12.4 1.3 copy.17
  13.7 0.0 all-gather.4.cloned.1.call-update
  13.7 0.0 all-gather.6.cloned.1.call-start
  13.8 55.5 %all-gather.4.cloned.1.call-done = bf16[32,256,256]{2,1,0:T(8,128)(2,1)} async-done(((bf16[8,256,256]{2,1,0:T(8,128)(2,1)}), bf16[32,256,256]{2,1,0:T(8,128)(2,1)}) %all-gather.4.cloned.1.call-update) | async-done | bytes 4194320 | tf_op jit(solution)/shard_map/all_gather | solution.py:120
  69.3 1.3 constant_dynamic-slice_fusion
  70.6 1.6 copy.20
  72.2 8.1 %all_gather.14 = bf16[32,256]{1,0:T(8,128)(2,1)S(1)} all-gather(bf16[8,256]{1,0:T(8,128)(2,1)S(1)} %get-tuple-element.9), channel_id=1, replica_groups=mesh['chan'=8,'win'=4] {'win'}, dimensions={0}, use_global_device_ids=true | all-gather | bytes 20480 | tf_op jit(solution)/shard_map/all_gather | solution.py:124
  80.3 0.1 dynamic-slice_bitcast_fusion
  80.4 14.4 %all-gather = bf16[8,64,32]{1,2,0:T(8,128)(2,1)S(1)} all-gather(bf16[1,64,32]{1,2,0:T(8,128)(2,1)S(1)} %dynamic-slice_bitcast_fusion), channel_id=1, replica_groups=mesh['chan'=8,'win'=4] {'chan'}, dimensions={0}, use_global_device_ids=true | all-gather | bytes 36864 | tf_op jit(solution)/shard_map/all_gather | solution.py:126
  94.8 0.1 reshape.26
  94.9 0.3 fusion.3
  95.2 1.2 broadcast_in_dim.2.scale_ref
  96.4 28.5 %copy.18 = bf16[32,256,256]{0,1,2:T(8,128)(2,1)} copy(bf16[32,256,256]{2,1,0:T(8,128)(2,1)} %all-gather.4.cloned.1.call-done) | data formatting | bytes 8388608 | tf_op jit(solution)/shard_map/all_gather | solution.py:120
  124.9 7.8 %fusion.5 = bf16[128,256,32]{2,1,0:T(8,128)(2,1)} fusion(bf16[128,2,256,32]{3,2,0,1:T(8,128)(2,1)} %bitcast.34), kind=kLoop, calls=%fused_computation.16 | loop fusion | flops 1048576 | bytes 4194304 | tf_op jit(solution)/shard_map/neg | solution.py:133
  132.7 7.1 %slice_bitcast_fusion = (bf16[128,256,32]{2,1,0:T(8,128)(2,1)S(1)}, bf16[128,256,32]{2,1,0:T(8,128)(2,1)S(1)}) fusion(bf16[128,2,256,32]{3,2,0,1:T(8,128)(2,1)} %bitcast.35), kind=kLoop, calls=%fused_computation.1 | loop fusion | bytes 8388608 | tf_op jit(solution)/shard_map/squeeze | solution.py:131
  139.9 1.2 copy-done
  141.1 11.3 %maximum_bitcast_fusion = (bf16[128,1,256,64]{3,2,1,0:T(8,128)(2,1)}, bf16[128,1,256,64]{3,2,1,0:T(8,128)(2,1)}) fusion(bf16[128,256,32]{2,1,0:T(8,128)(2,1)S(1)} %get-tuple-element.5, bf16[128,256,32]{2,1,0:T(8,128)(2,1)S(1)} %get-tuple-element.6, bf16[128,256,32]{2,1,0:T(8,128)(2,1)S(1)} %copy-done), kind=kLoop, calls=%fused_computation.3 | loop fusion | flops 16777216 | bytes 14680064 | tf_op jit(solution)/shard_map/stack | solution.py:132
  152.4 14.5 %pad_maximum_fusion.src_ref = bf16[128,2,256,64]{3,2,1,0:T(8,128)(2,1)} fusion(bf16[128,1,256,64]{3,2,1,0:T(8,128)(2,1)} %get-tuple-element.8, bf16[128,1,256,64]{3,2,1,0:T(8,128)(2,1)} %get-tuple-element.7), kind=kLoop, calls=%fused_computation | loop fusion | flops 4194304 | bytes 16777216 | tf_op jit(solution)/shard_map/stack | solution.py:132
  166.9 12.5 %reshape.23 = bf16[32,512,2,128]{3,2,0,1:T(2,128)(2,1)} reshape(bf16[32,512,256]{2,0,1:T(8,128)(2,1)} %all-gather.6.cloned.1.call-done) | data formatting | bytes 16777216 | tf_op jit(solution)/shard_map/reshape | solution.py:136
  179.4 16.8 %copy.21 = bf16[32,512,2,128]{1,0,2,3:T(8,128)(2,1)} copy(bf16[32,512,2,128]{3,2,0,1:T(2,128)(2,1)} %reshape.23) | data formatting | bytes 16777216 | tf_op jit(solution)/shard_map/reshape | solution.py:136
  196.2 204.3 %pairs.1 = f32[256,8,1,64,128]{4,3,2,1,0:T(8,128)} custom-call(bf16[128,2,256,64]{3,2,1,0:T(8,128)(2,1)} %pad_maximum_fusion.src_ref, bf16[128,64,512]{2,1,0:T(8,128)(2,1)} %bitcast.36, f32[256,1,512]{2,1,0:T(1,128)} %broadcast_in_dim.2.scale_ref, bf16[256,128]{1,0:T(8,128)(2,1)} %constant.24.clone.inv_ref), custom_call_target="tpu_custom_call" | custom-call | flops 12884901888 | bytes 67108864 | tf_op jit(solution)/shard_map/pairs/pallas_call | solution.py:76
  (6 shorter events, 0.1 us)
Async XLA Ops:
  6.5 62.8 %all-gather.4.cloned.1.call-start = ((), (), s32[]{:S(2)}) async-start(), calls=%async_computation | async-start | bytes 5242880 | tf_op jit(solution)/shard_map/all_gather | solution.py:120
  13.7 153.1 %all-gather.6.cloned.1.call-start = ((), (), s32[]{:S(2)}) async-start(), calls=%async_computation.1 | async-start | bytes 9437184 | tf_op jit(solution)/shard_map/all_gather | solution.py:123
  132.7 8.4 %copy-start = (bf16[128,256,32]{2,1,0:T(8,128)(2,1)S(1)}, bf16[128,256,32]{2,1,0:T(8,128)(2,1)}, u32[]{:S(2)}) copy-start(bf16[128,256,32]{2,1,0:T(8,128)(2,1)} %fusion.5) | copy-start | bytes 6291460
Sparse Core Ops, SparseCore 0:
  13.9 55.3 all-gather.3
  72.3 82.4 all-gather.5
where the time goes:
time: 408 us; the launch traced here: 407 us
  Pallas kernels  204 us (50%)
  local copies, waits for them, and re-layouts  71.7 us (18%)
  waiting for transfers between devices  55.5 us (14%)
  other arithmetic  34.7 us (9%)
  blocking collectives  22.5 us (6%)
  between operations  13.5 us (3%)
  matrix products  5.1 us (1%)
    pallas_call x1, Pallas kernels, pair_block(): pl.pallas_call(pair_kernel, grid=(receivers // ti, sources // sc), in_spe...  204 us
    all_gather x1, waiting for transfers between devices, on_device(): src = lax.all_gather(whitened, 'win', axis=0, tiled=True)  55.5 us
    reshape x2, local copies, waits for them, and re-layouts, on_device(): recv_r = recv.reshape(windows, receivers, 2, BINS).transpose(3, 2, 0, 1)  29.3 us
    all_gather x1, local copies, waits for them, and re-layouts, on_device(): src = lax.all_gather(whitened, 'win', axis=0, tiled=True)  28.5 us
    another operation x2, other arithmetic, on_device(): jnp.stack([jnp.concatenate([real, imag], -1), jnp.concatenate([-imag, rea...  25.8 us
    all_gather x1, blocking collectives, on_device(): recv_flags = lax.all_gather(own_flags, 'chan', axis=1, tiled=True)  14.4 us
  transfers between devices with their start and end apart: 2, of which 1 were waited for; matrix products, arithmetic and copies ran while one was open for 17% of the time, Pallas kernels for 0%

commit v1 on v0

--- a/solution.py
+++ b/solution.py
@@ -117,24 +117,23 @@
     slot = channels // slots
     v = lax.axis_index("win")
 
-    src = lax.all_gather(whitened, "win", axis=0, tiled=True)
-    windows = src.shape[0]
-    own = lax.dynamic_slice_in_dim(src, v * slot, slot, axis=1)
-    recv = lax.all_gather(own, "chan", axis=1, tiled=True)
+    local = whitened.reshape(win_rows, channels, 2, BINS).transpose(3, 2, 0, 1)
+    local = local.reshape(BINS, 2 * win_rows, channels)
+    src = lax.all_gather(local, "win", axis=1, tiled=True)
+    depth = src.shape[1]
+    own = lax.dynamic_slice_in_dim(src, v * slot, slot, axis=2)
+    recv = lax.all_gather(own, "chan", axis=0)
     src_flags = lax.all_gather(flags, "win", axis=0, tiled=True)
     own_flags = lax.dynamic_slice_in_dim(src_flags, v * slot, slot, axis=1)
     recv_flags = lax.all_gather(own_flags, "chan", axis=1, tiled=True)
     count = jnp.einsum("ws,wi->si", src_flags, recv_flags, preferred_element_type=jnp.float32)
     scale = 1.0 / jnp.maximum(count, 1.0)
 
-    s4 = src.reshape(windows, channels, 2, BINS).transpose(3, 2, 1, 0)
-    real, imag = s4[:, 0], s4[:, 1]
-    src_l = jnp.stack(
-        [jnp.concatenate([real, imag], -1), jnp.concatenate([-imag, real], -1)], axis=1
-    )
-    receivers = blocks * slot
-    recv_r = recv.reshape(windows, receivers, 2, BINS).transpose(3, 2, 0, 1)
-    recv_r = recv_r.reshape(BINS, 2 * windows, receivers)
+    parts = src.reshape(BINS, slots, 2, win_rows, channels)
+    turned = jnp.concatenate([-parts[:, :, 1:], parts[:, :, :1]], axis=2)
+    both = jnp.stack([src, turned.reshape(BINS, depth, channels)], axis=1)
+    src_l = jnp.swapaxes(both, 2, 3)
+    recv_r = jnp.transpose(recv, (1, 2, 0, 3)).reshape(BINS, depth, blocks * slot)
     return pair_block(src_l, recv_r, scale, jnp.asarray(inverse), slot)
 
 

time: 408 us -> 400 us (0.980)
  other arithmetic: 34.7 us -> 18.2 us
  waiting for transfers between devices: 55.5 us -> 69.7 us
  local copies, waits for them, and re-layouts: 71.7 us -> 60.5 us
  blocking collectives: 22.5 us -> 27.7 us
    another operation x2 -> x0, other arithmetic: 25.8 us -> none  [on_device(): jnp.stack([jnp.concatenate([real, imag], -1), jnp.concatenate([-imag, rea...]
    reshape x2 -> x3, local copies, waits for them, and re-layouts: 29.3 us -> 14.6 us  [the longest x1 12.7 us: on_device(): jnp.transpose(recv, (1, 2, 0, 3)).reshape(BINS, depth, blocks * slot)]
    transpose x0 -> x1, other arithmetic: none -> 14.6 us  [on_device(): src_l = jnp.swapaxes(both, 2, 3)]
    all_gather x1 -> x2, local copies, waits for them, and re-layouts: 28.5 us -> 14 us  [on_device(): src = lax.all_gather(local, 'win', axis=1, tiled=True)]
    all_gather x2, waiting for transfers between devices: 55.5 us -> 69.6 us  [the longest x1 55.5 us: on_device(): src = lax.all_gather(local, 'win', axis=1, tiled=True)]
    transpose x0 -> x1, local copies, waits for them, and re-layouts: none -> 9.31 us  [on_device(): jnp.transpose(recv, (1, 2, 0, 3)).reshape(BINS, depth, blocks * slot)]
    another operation x0 -> x1, local copies, waits for them, and re-layouts: none -> 8.41 us  [on_device(): both = jnp.stack([src, turned.reshape(BINS, depth, channels)], axis=1)]
    unnamed x4 -> x3, local copies, waits for them, and re-layouts: 1.4 us -> 9.14 us
  transfers between devices with their start and end apart: 2 -> 2, of which waited for: 1 -> 2; matrix products, arithmetic and copies ran while one was open for 17% -> 10% of each run, Pallas kernels for 0% -> 0%
where the time goes in v1:
time: 400 us; the launch traced here: 399 us
  Pallas kernels  204 us (51%)
  waiting for transfers between devices  69.7 us (17%)
  local copies, waits for them, and re-layouts  60.5 us (15%)
  blocking collectives  27.7 us (7%)
  other arithmetic  18.2 us (5%)
  between operations  13.5 us (3%)
  matrix products  5.1 us (1%)
    pallas_call x1, Pallas kernels, pair_block(): pl.pallas_call(pair_kernel, grid=(receivers // ti, sources // sc), in_spe...  204 us
    all_gather x1, waiting for transfers between devices, on_device(): src = lax.all_gather(local, 'win', axis=1, tiled=True)  55.5 us
    all_gather x1, blocking collectives, on_device(): recv_flags = lax.all_gather(own_flags, 'chan', axis=1, tiled=True)  19.6 us
    transpose x1, other arithmetic, on_device(): src_l = jnp.swapaxes(both, 2, 3)  14.6 us
    all_gather x1, waiting for transfers between devices, on_device(): recv = lax.all_gather(own, 'chan', axis=0)  14.1 us
    all_gather x2, local copies, waits for them, and re-layouts, on_device(): src = lax.all_gather(local, 'win', axis=1, tiled=True)  14 us
    reshape x1, local copies, waits for them, and re-layouts, on_device(): jnp.transpose(recv, (1, 2, 0, 3)).reshape(BINS, depth, blocks * slot)  12.7 us
    transpose x1, local copies, waits for them, and re-layouts, on_device(): jnp.transpose(recv, (1, 2, 0, 3)).reshape(BINS, depth, blocks * slot)  9.31 us
  transfers between devices with their start and end apart: 2, of which 2 were waited for; matrix products, arithmetic and copies ran while one was open for 10% of the time, Pallas kernels for 0%

profile of v1, /device:TPU:0, one launch (start us, length us, event | category | flops | bytes accessed | tf_op | source)
XLA Modules:
  0.0 399.1 jit_solution(17277720253808780195)
XLA Ops:
  6.5 0.8 fusion.4
  7.3 4.8 %multiply_reduce_fusion = (f32[8,256]{1,0:T(8,128)S(1)}, f32[256,8,256]{2,0,1:T(8,128)S(1)}) fusion(bf16[1500,256,1]{1,0,2:T(8,128)(2,1)} %constant.25, bf16[8,256,1500]{1,0,2:T(8,128)(2,1)} %param.4), kind=kOutput, calls=%fused_computation.6 | convolution fusion | flops 1573910528 | bytes 9017344 | tf_op jit(solution)/shard_map/dot_general | solution.py:105
  12.2 0.2 multiply_convert_fusion
  12.4 0.6 copy.46
  13.0 1.3 copy.30
  14.4 55.5 %all-gather.5.cloned.1.call-done = bf16[128,64,256]{2,0,1:T(8,128)(2,1)} async-done(((bf16[128,16,256]{2,0,1:T(8,128)(2,1)}), bf16[128,64,256]{2,0,1:T(8,128)(2,1)}) %all-gather.5.cloned.1.call-update) | async-done | bytes 4194320 | tf_op jit(solution)/shard_map/all_gather | solution.py:122
  69.9 2.3 constant_dynamic-slice_fusion
  72.2 1.6 copy.34
  73.8 8.1 %all_gather.18 = bf16[32,256]{1,0:T(8,128)(2,1)S(1)} all-gather(bf16[8,256]{1,0:T(8,128)(2,1)S(1)} %get-tuple-element.7), channel_id=1, replica_groups=mesh['chan'=8,'win'=4] {'win'}, dimensions={0}, use_global_device_ids=true | all-gather | bytes 20480 | tf_op jit(solution)/shard_map/all_gather | solution.py:126
  82.0 19.6 %all-gather.1 = bf16[8,64,32]{1,2,0:T(8,128)(2,1)S(1)} all-gather(bf16[1,64,32]{1,2,0:T(8,128)(2,1)S(1)} %dynamic-slice_bitcast_fusion), channel_id=1, replica_groups=mesh['chan'=8,'win'=4] {'chan'}, dimensions={0}, use_global_device_ids=true | all-gather | bytes 36864 | tf_op jit(solution)/shard_map/all_gather | solution.py:128
  101.7 0.1 reshape.31
  101.8 0.3 fusion.3
  102.1 1.2 broadcast_in_dim.2.scale_ref
  103.3 4.6 %copy.32 = bf16[128,64,256]{2,1,0:T(8,128)(2,1)S(1)} copy(bf16[128,64,256]{2,0,1:T(8,128)(2,1)} %all-gather.5.cloned.1.call-done) | data formatting | bytes 8388608 | tf_op jit(solution)/shard_map/all_gather | solution.py:122
  107.8 0.3 slice_negate_fusion
  108.1 2.3 pad_maximum_fusion
  110.4 8.4 %copy.33 = bf16[128,1,64,256]{2,3,1,0:T(8,128)(2,1)} copy(bf16[128,1,64,256]{3,2,0,1:T(8,128)(2,1)} %bitcast.37) | data formatting | bytes 8388608 | tf_op jit(solution)/shard_map/stack;reshape | solution.py:134
  118.8 9.4 %copy.31 = bf16[128,64,256]{1,2,0:T(8,128)(2,1)} copy(bf16[128,64,256]{2,0,1:T(8,128)(2,1)} %all-gather.5.cloned.1.call-done) | data formatting | bytes 8388608 | tf_op jit(solution)/shard_map/all_gather | solution.py:122
  128.3 14.6 %maximum_bitcast_fusion.src_ref = bf16[128,2,256,64]{3,2,1,0:T(8,128)(2,1)} fusion(bf16[128,1,64,256]{2,3,1,0:T(8,128)(2,1)} %copy.33, bf16[128,1,64,256]{2,3,1,0:T(8,128)(2,1)} %bitcast.36), kind=kLoop, calls=%fused_computation | loop fusion | flops 4194304 | bytes 16777216 | tf_op jit(solution)/shard_map/transpose | solution.py:135
  142.8 14.1 %all-gather.7.cloned.1.call-done = bf16[1024,64,64]{0,2,1:T(8,128)(2,1)} async-done(((bf16[128,64,64]{0,2,1:T(8,128)(2,1)}), bf16[1024,64,64]{0,2,1:T(8,128)(2,1)}) %all-gather.7.cloned.1.call-update) | async-done | bytes 8388624 | tf_op jit(solution)/shard_map/all_gather | solution.py:125
  157.0 8.9 %copy.40 = bf16[512,8,8,128]{3,2,1,0:T(8,128)(2,1)} copy(bf16[512,8,8,128]{3,1,2,0:T(8,128)(2,1)} %bitcast.39) | data formatting | bytes 16777216
  165.9 9.3 %copy.35 = bf16[128,64,8,64]{0,3,2,1:T(8,128)(2,1)} copy(bf16[128,64,8,64]{0,2,3,1:T(8,128)(2,1)} %bitcast.34) | data formatting | bytes 16777216 | tf_op jit(solution)/shard_map/transpose | solution.py:136
  175.2 12.7 %copy.38.recv_ref = bf16[128,64,512]{2,1,0:T(8,128)(2,1)} copy(bf16[128,64,512]{0,2,1:T(8,128)(2,1)} %bitcast.35) | data formatting | bytes 16777216 | tf_op jit(solution)/shard_map/reshape | solution.py:136
  187.9 204.3 %pairs.1 = f32[256,8,1,64,128]{4,3,2,1,0:T(8,128)} custom-call(bf16[128,2,256,64]{3,2,1,0:T(8,128)(2,1)} %maximum_bitcast_fusion.src_ref, bf16[128,64,512]{2,1,0:T(8,128)(2,1)} %copy.38.recv_ref, f32[256,1,512]{2,1,0:T(1,128)} %broadcast_in_dim.2.scale_ref, bf16[256,128]{1,0:T(8,128)(2,1)} %constant.24.clone.inv_ref), custom_call_target="tpu_custom_call" | custom-call | flops 12884901888 | bytes 67108864 | tf_op jit(solution)/shard_map/pairs/pallas_call | solution.py:76
  (7 shorter events, 0.2 us)
Async XLA Ops:
  6.5 63.4 %all-gather.5.cloned.1.call-start = ((), (), s32[]{:S(2)}) async-start(), calls=%async_computation | async-start | bytes 5242880 | tf_op jit(solution)/shard_map/all_gather | solution.py:122
  14.3 142.6 %all-gather.7.cloned.1.call-start = ((), (), s32[]{:S(2)}) async-start(), calls=%async_computation.1 | async-start | bytes 9437184 | tf_op jit(solution)/shard_map/all_gather | solution.py:125
Sparse Core Ops, SparseCore 0:
  14.5 55.3 all-gather.4
  74.0 82.9 all-gather.6
